TPU v7x, 32 devices: a whole 2x2x4 slice. The times are simulated.
32 devices in a mesh: tracer: 4 (over z), gx: 2 (over x), gy: 4 (over y, core).
Axes of the slice: x: 2, y: 2, z: 4, core: 2. Of those that a mesh axis runs over, the one named last changes fastest.
Arguments:
- tracers: float32 [32, 4, 64, 512], P('tracer', None, 'gx', 'gy'), may hold values from -4 to 4
- air_mass: float32 [2, 4, 64, 512], P(None, 'tracer', 'gx', 'gy'), may hold values from 2 to 4
- flux_x: float32 [2, 4, 64, 512], P(None, 'tracer', 'gx', 'gy'), may hold values from -0.4 to 0.4
- flux_y: float32 [2, 4, 64, 512], P(None, 'tracer', 'gx', 'gy'), may hold values from -0.4 to 0.4
Outputs:
- advected: float32 [32, 4, 64, 512], P('tracer', None, 'gx', 'gy')
All inputs are finite; a program needn't handle non-finite values.
Results may differ from a plain program's by a relative error of at most 0.0003.
Values sent between devices are 32-bit elements; how exact they have to be, the bound alone decides.
A program may use at most 64 MiB of HBM per device.

v0:
```python
import functools

import jax
import jax.numpy as jnp
from jax import lax
from jax.experimental import pallas as pl
from jax.experimental.pallas import tpu as pltpu
from jax.sharding import PartitionSpec as P

MESH = pl.DeviceIdType.MESH
LANES = 128
SUB = 8


def sweep(q, face, cell, put, begin, end):
    steps, devs, limited, fluxes, rows = {}, {}, {}, {}, {}

    def Q(i):
        if i not in rows:
            rows[i] = q(i)
        return rows[i]

    def D(k):
        if k not in steps:
            steps[k] = Q(k) - Q(k - 1)
        return steps[k]

    def right_of(k):
        if k not in devs:
            raw = 0.5 * D(k) + (1.0 / 12.0) * (D(k - 1) - D(k + 1))
            devs[k] = jnp.minimum(jnp.maximum(raw, jnp.minimum(D(k), 0.0)), jnp.maximum(D(k), 0.0))
        return devs[k]

    def lim(i):
        if i not in limited:
            left, right = D(i) - right_of(i), right_of(i + 1)
            left2, right2 = left + left, right + right
            limited[i] = (
                jnp.minimum(jnp.maximum(left, jnp.minimum(right2, 0.0)), jnp.maximum(right2, 0.0)),
                jnp.minimum(jnp.maximum(right, jnp.minimum(left2, 0.0)), jnp.maximum(left2, 0.0)),
            )
        return limited[i]

    def G(k):
        if k not in fluxes:
            f, near_w, far_w = face(k)
            east = f >= 0.0
            (l0, r0), (l1, r1) = lim(k - 1), lim(k)
            fluxes[k] = (
                f * jnp.where(east, Q(k - 1), Q(k))
                + near_w * jnp.where(east, r0, l1)
                + far_w * jnp.where(east, l0, r1)
            )
        return fluxes[k]

    for i in range(begin, end):
        alpha, beta = cell(i)
        put(i, alpha * Q(i) - beta * (G(i + 1) - G(i)))


def face_weights(f, mass_left, mass_right):
    size = jnp.abs(f)
    c = size / jnp.where(f >= 0.0, mass_left, mass_right)
    rest = 1.0 - c
    part = size * rest
    return part * rest, part * c


def kernel(n_lev, n_x, n_y, steps, tl, nlon, x_ref, m_ref, fx_ref, fy_ref, o_ref,
           dyn, eout, ein, edge, hxo, hxi, hyo, hyi, xs, qx, yb, yo,
           cf, cp, cq, ca, cb, mp, fp, mxs, myp, fyp, yp, yq, ya, ybt,
           d_s, d_r, ea_s, ea_r, eb_s, eb_r, hx_s, hx_r, hy_s, hy_r):
    z, gx, gy = lax.axis_index("tracer"), lax.axis_index("gx"), lax.axis_index("gy")
    peers = [lax.rem(z + d, n_lev) for d in range(1, n_lev)]
    left, right = lax.rem(gx + n_x - 1, n_x), lax.rem(gx + 1, n_x)
    south, north = lax.rem(gy + n_y - 1, n_y), lax.rem(gy + 1, n_y)
    H = 3
    nl = n_lev * nlon

    barrier = pltpu.get_barrier_semaphore()
    who = [{"tracer": p} for p in peers] + [{"gx": left}, {"gx": right}, {"gy": south}, {"gy": north}]
    for w in who:
        pl.semaphore_signal(barrier, inc=1, device_id=w, device_id_type=MESH)

    def remote(src, dst, ss, rs, to):
        return pltpu.make_async_remote_copy(src_ref=src, dst_ref=dst, send_sem=ss, recv_sem=rs,
                                            device_id=to, device_id_type=MESH)

    def pack_x(s, src):
        def body(lev, _):
            for c in range(H):
                to = pl.ds(pl.multiple_of((lev * H + c) * SUB, SUB), SUB)
                hxo[s, 0, to, :] = src[pl.ds(lev * nlon + c, SUB, stride=nl), :]
                hxo[s, 1, to, :] = src[pl.ds(lev * nlon + nlon - H + c, SUB, stride=nl), :]
            return 0
        lax.fori_loop(0, n_lev, body, 0)

    for s in range(steps):
        for f, ref in enumerate((m_ref, fx_ref, fy_ref)):
            dyn[s * n_lev + z, f * nlon:(f + 1) * nlon, :] = ref[s * nlon:(s + 1) * nlon, :]
        eout[s * 4:s * 4 + 1, :] = m_ref[(s + 1) * nlon - 1:(s + 1) * nlon, :]
        eout[s * 4 + 1:s * 4 + 2, :] = m_ref[s * nlon:s * nlon + 1, :]
        eout[s * 4 + 2:s * 4 + 3, :] = fx_ref[s * nlon:s * nlon + 1, :]
        eout[s * 4 + 3:s * 4 + 4, :] = fx_ref[s * nlon:s * nlon + 1, :]
    pack_x(0, x_ref)
    pl.semaphore_wait(barrier, len(who))

    pending = []

    def go(copy):
        copy.start()
        pending.append(copy)

    go(remote(eout, ein.at[1], ea_s.at[0], ea_r.at[1], {"gx": left}))
    go(remote(eout, ein.at[0], ea_s.at[1], ea_r.at[0], {"gx": right}))

    def send_dyn(s):
        for d, p in enumerate(peers):
            go(remote(dyn.at[s * n_lev + z], dyn.at[s * n_lev + z], d_s.at[s, d], d_r.at[s, z], {"tracer": p}))

    def send_x(s):
        go(remote(hxo.at[s, 0], hxi.at[s, 1], hx_s.at[s, 0], hx_r.at[s, 1], {"gx": left}))
        go(remote(hxo.at[s, 1], hxi.at[s, 0], hx_s.at[s, 1], hx_r.at[s, 0], {"gx": right}))

    send_dyn(0)
    send_x(0)
    for side in range(2):
        remote(eout, ein.at[side], ea_s.at[side], ea_r.at[side], {"gx": left}).wait_recv()
    for s in range(steps):
        edge[z, s * 4:s * 4 + 1, :] = ein[0, s * 4:s * 4 + 1, :]
        edge[z, s * 4 + 1:s * 4 + 4, :] = ein[1, s * 4 + 1:s * 4 + 4, :]
    for d, p in enumerate(peers):
        go(remote(edge.at[z], edge.at[z], eb_s.at[d], eb_r.at[z], {"tracer": p}))
    for s in range(1, steps):
        send_dyn(s)

    for s in range(steps):
        src = x_ref if s == 0 else xs
        dst = xs if s < steps - 1 else o_ref

        def x_inner(j, _):
            lev = lax.rem(z + j, n_lev)
            slot = s * n_lev + lev

            @pl.when(j > 0)
            def _():
                remote(dyn.at[slot], dyn.at[slot], d_s.at[s, 0], d_r.at[s, lev], {"tracer": z}).wait_recv()
                if s == 0:
                    remote(edge.at[lev], edge.at[lev], eb_s.at[0], eb_r.at[lev], {"tracer": z}).wait_recv()

            m = dyn[slot, 0:nlon, :]
            mp[SUB:SUB + nlon, :] = m
            mp[0:SUB, :] = jnp.broadcast_to(edge[lev, s * 4:s * 4 + 1, :], (SUB, LANES))
            mp[SUB + nlon:2 * SUB + nlon, :] = jnp.broadcast_to(edge[lev, s * 4 + 1:s * 4 + 2, :], (SUB, LANES))
            fp[0:nlon, :] = dyn[slot, nlon:2 * nlon, :]
            fp[nlon:nlon + SUB, :] = jnp.broadcast_to(edge[lev, s * 4 + 2:s * 4 + 3, :], (SUB, LANES))
            f = fp[0:nlon + SUB, :]
            pw, qw = face_weights(f, mp[SUB - 1:2 * SUB - 1 + nlon, :], mp[SUB:2 * SUB + nlon, :])
            cf[lev] = f
            cp[lev] = pw
            cq[lev] = qw
            mx = m - (fp[1:nlon + 1, :] - fp[0:nlon, :])
            inv = 1.0 / mx
            ca[lev] = m * inv
            cb[lev] = inv
            mxs[pl.ds(pl.multiple_of(lev * nlon, nlon), nlon), :] = mx
            base = lev * nlon
            sweep(
                lambda i: src[pl.ds(base + i, SUB, stride=nl), :],
                lambda k: (cf[lev, k:k + 1, :], cp[lev, k:k + 1, :], cq[lev, k:k + 1, :]),
                lambda i: (ca[lev, i:i + 1, :], cb[lev, i:i + 1, :]),
                functools.partial(put_x, base), H, nlon - H)
            return 0

        def put_x(base, i, v):
            qx[pl.ds(base + i, SUB, stride=nl), :] = v

        lax.fori_loop(0, n_lev, x_inner, 0)
        for side in range(2):
            remote(hxo.at[s, 0], hxi.at[s, side], hx_s.at[s, side], hx_r.at[s, side], {"gx": left}).wait_recv()

        def x_edge(lev, _):
            base = lev * nlon

            def q(i):
                if i < 0:
                    return hxi[s, 0, pl.ds(pl.multiple_of((lev * H + i + H) * SUB, SUB), SUB), :]
                if i >= nlon:
                    return hxi[s, 1, pl.ds(pl.multiple_of((lev * H + i - nlon) * SUB, SUB), SUB), :]
                return src[pl.ds(base + i, SUB, stride=nl), :]

            for a, b in ((0, H), (nlon - H, nlon)):
                sweep(
                    q,
                    lambda k: (cf[lev, k:k + 1, :], cp[lev, k:k + 1, :], cq[lev, k:k + 1, :]),
                    lambda i: (ca[lev, i:i + 1, :], cb[lev, i:i + 1, :]),
                    functools.partial(put_x, base), a, b)
            return 0

        lax.fori_loop(0, n_lev, x_edge, 0)

        off = H * SUB

        def turn(t, _):
            yb[pl.ds(off + t, LANES, stride=SUB), :] = jnp.transpose(
                qx[pl.ds(pl.multiple_of(t * nl, nl), nl), :])
            return 0
        lax.fori_loop(0, SUB, turn, 0)
        mt = jnp.transpose(mxs[...])
        ft = jnp.transpose(jnp.concatenate(
            [dyn[s * n_lev + lev, 2 * nlon:3 * nlon, :] for lev in range(n_lev)], axis=0))
        myp[SUB:SUB + LANES, :] = mt
        fyp[0:LANES, :] = ft
        extra = jnp.concatenate([mt[0:1], mt[LANES - 1:LANES], ft[0:1], ft[0:1], ft[0:1], ft[0:1], ft[0:1], ft[0:1]], axis=0)
        for side in range(2):
            hyo[s, side, H * SUB:(H + 1) * SUB, :] = extra
        hyo[s, 0, 0:H * SUB, :] = yb[off:off + H * SUB, :]
        hyo[s, 1, 0:H * SUB, :] = yb[off + (LANES - H) * SUB:off + LANES * SUB, :]
        go(remote(hyo.at[s, 0], hyi.at[s, 1], hy_s.at[s, 0], hy_r.at[s, 1], {"gy": south}))
        go(remote(hyo.at[s, 1], hyi.at[s, 0], hy_s.at[s, 1], hy_r.at[s, 0], {"gy": north}))

        f = fyp[SUB:LANES, :]
        pw, qw = face_weights(f, myp[2 * SUB - 1:SUB + LANES - 1, :], myp[2 * SUB:SUB + LANES, :])
        yp[SUB:LANES, :] = pw
        yq[SUB:LANES, :] = qw
        m = myp[SUB:LANES, :]
        inv = 1.0 / (m - (fyp[1:LANES - SUB + 1, :] - fyp[0:LANES - SUB, :]))
        ya[0:LANES - SUB, :] = m * inv
        ybt[0:LANES - SUB, :] = inv

        def y_rows(first, count):
            sweep(
                lambda i: yb[pl.ds(pl.multiple_of(off + (first + i) * SUB, SUB), SUB), :],
                lambda k: (fyp[pl.ds(first + k, 1), :], yp[pl.ds(first + k, 1), :], yq[pl.ds(first + k, 1), :]),
                lambda i: (ya[pl.ds(first + i, 1), :], ybt[pl.ds(first + i, 1), :]),
                put_y(first), 0, count)

        def put_y(first):
            def put(i, v):
                yo[pl.ds(pl.multiple_of((first + i) * SUB, SUB), SUB), :] = v
            return put

        def y_inner(b, _):
            y_rows(SUB + b * 16, 16)
            return 0
        lax.fori_loop(0, (LANES - 2 * SUB) // 16, y_inner, 0)

        for side in range(2):
            remote(hyo.at[s, 0], hyi.at[s, side], hy_s.at[s, side], hy_r.at[s, side], {"gy": south}).wait_recv()
        at_south, at_north = gy == 0, gy == n_y - 1
        yb[0:H * SUB, :] = jnp.where(at_south, 0.0, hyi[s, 0, 0:H * SUB, :])
        yb[off + LANES * SUB:off + (LANES + H) * SUB, :] = jnp.where(at_north, 0.0, hyi[s, 1, 0:H * SUB, :])
        e = H * SUB
        myp[0:SUB, :] = jnp.broadcast_to(jnp.where(at_south, 1.0, hyi[s, 0, e + 1:e + 2, :]), (SUB, LANES))
        myp[SUB + LANES:2 * SUB + LANES, :] = jnp.broadcast_to(
            jnp.where(at_north, 1.0, hyi[s, 1, e:e + 1, :]), (SUB, LANES))
        fyp[LANES:LANES + SUB, :] = jnp.broadcast_to(
            jnp.where(at_north, 0.0, hyi[s, 1, e + 2:e + 3, :]), (SUB, LANES))
        fyp[0:1, :] = jnp.where(at_south, 0.0, fyp[0:1, :])
        for a in (0, LANES):
            f = fyp[a:a + SUB, :]
            pw, qw = face_weights(f, myp[a + SUB - 1:a + 2 * SUB - 1, :], myp[a + SUB:a + 2 * SUB, :])
            yp[a:a + SUB, :] = pw
            yq[a:a + SUB, :] = qw
        for a in (0, LANES - SUB):
            m = myp[a + SUB:a + 2 * SUB, :]
            inv = 1.0 / (m - (fyp[a + 1:a + SUB + 1, :] - fyp[a:a + SUB, :]))
            ya[a:a + SUB, :] = m * inv
            ybt[a:a + SUB, :] = inv

        def y_edge(b, _):
            y_rows(b * (LANES - SUB), SUB)
            return 0
        lax.fori_loop(0, 2, y_edge, 0)

        def back(t, _):
            dst[pl.ds(pl.multiple_of(t * nl, nl), nl), :] = jnp.transpose(yo[pl.ds(t, LANES, stride=SUB), :])
            return 0
        lax.fori_loop(0, SUB, back, 0)
        if s < steps - 1:
            pack_x(s + 1, xs)
            send_x(s + 1)

    for copy in pending:
        copy.wait_send()


def on_device(tracers, air_mass, flux_x, flux_y):
    nt, nlev, nlon, nlat = tracers.shape
    steps, tl = air_mass.shape[:2]
    n_lev, n_x, n_y = lax.axis_size("tracer"), lax.axis_size("gx"), lax.axis_size("gy")
    assert nt == SUB and nlat == LANES and nlev * nlon == LANES and tl == 1 and steps * 4 <= SUB
    rows = nt * nlev * nlon
    V = lambda *shape: pltpu.VMEM(shape, jnp.float32)
    dma = lambda *shape: pltpu.SemaphoreType.DMA(shape)
    H = 3
    out = pl.pallas_call(
        functools.partial(kernel, n_lev, n_x, n_y, steps, tl, nlon),
        out_shape=jax.ShapeDtypeStruct((rows, LANES), jnp.float32),
        in_specs=[pl.BlockSpec(memory_space=pltpu.VMEM)] * 4,
        out_specs=pl.BlockSpec(memory_space=pltpu.VMEM),
        scratch_shapes=[
            V(steps * n_lev, 3 * nlon, LANES),
            V(SUB, LANES), V(2, SUB, LANES), V(n_lev, SUB, LANES),
            V(steps, 2, n_lev * H * SUB, LANES), V(steps, 2, n_lev * H * SUB, LANES),
            V(steps, 2, (H + 1) * SUB, LANES), V(steps, 2, (H + 1) * SUB, LANES),
            V(rows, LANES), V(rows, LANES), V((LANES + 2 * H) * SUB, LANES), V(LANES * SUB, LANES),
            V(n_lev, nlon + SUB, LANES), V(n_lev, nlon + SUB, LANES), V(n_lev, nlon + SUB, LANES),
            V(n_lev, nlon, LANES), V(n_lev, nlon, LANES),
            V(nlon + 2 * SUB, LANES), V(nlon + SUB, LANES), V(LANES, LANES),
            V(LANES + 2 * SUB, LANES), V(LANES + SUB, LANES), V(LANES + SUB, LANES), V(LANES + SUB, LANES),
            V(LANES, LANES), V(LANES, LANES),
            dma(steps, n_lev), dma(steps, n_lev), dma(2), dma(2), dma(n_lev), dma(n_lev),
            dma(steps, 2), dma(steps, 2), dma(steps, 2), dma(steps, 2),
        ],
        compiler_params=pltpu.CompilerParams(
            collective_id=0, has_side_effects=True, vmem_limit_bytes=32 * 1024 * 1024),
    )(tracers.reshape(rows, LANES), air_mass.reshape(-1, LANES), flux_x.reshape(-1, LANES), flux_y.reshape(-1, LANES))
    return out.reshape(tracers.shape)


def solution(mesh):
    in_specs = (
        P("tracer", None, "gx", "gy"),
        P(None, "tracer", "gx", "gy"),
        P(None, "tracer", "gx", "gy"),
        P(None, "tracer", "gx", "gy"),
    )
    out_specs = P("tracer", None, "gx", "gy")
    return jax.shard_map(
        on_device, mesh=mesh, in_specs=in_specs, out_specs=out_specs, check_vma=False
    )
```

profile of v0, /device:TPU:0, one launch (start us, length us, event | category | flops | bytes accessed | tf_op | source)
XLA Modules:
  0.0 30.7 jit_solution(6962040273889621778)
XLA Ops:
  0.0 0.0 copy-start
  0.0 1.0 %copy-done = f32[8,4,32,128]{3,2,1,0:T(8,128)S(1)} copy-done((f32[8,4,32,128]{3,2,1,0:T(8,128)S(1)}, f32[8,4,32,128]{3,2,1,0:T(8,128)}, u32[]{:S(2)}) %copy-start) | copy-done | bytes 524312
  1.0 0.0 copy-start.1
  1.0 0.8 %copy-done.1 = f32[2,1,32,128]{3,2,1,0:T(8,128)S(1)} copy-done((f32[2,1,32,128]{3,2,1,0:T(8,128)S(1)}, f32[2,1,32,128]{3,2,1,0:T(8,128)}, u32[]{:S(2)}) %copy-start.1) | copy-done | bytes 32792
  1.8 0.0 copy-start.2
  1.8 0.8 %copy-done.2 = f32[2,1,32,128]{3,2,1,0:T(8,128)S(1)} copy-done((f32[2,1,32,128]{3,2,1,0:T(8,128)S(1)}, f32[2,1,32,128]{3,2,1,0:T(8,128)}, u32[]{:S(2)}) %copy-start.2) | copy-done | bytes 32792
  2.6 0.0 copy-start.3
  2.6 0.8 %copy-done.3 = f32[2,1,32,128]{3,2,1,0:T(8,128)S(1)} copy-done((f32[2,1,32,128]{3,2,1,0:T(8,128)S(1)}, f32[2,1,32,128]{3,2,1,0:T(8,128)}, u32[]{:S(2)}) %copy-start.3) | copy-done | bytes 32792
  3.3 26.6 %shard_map.46 = f32[1024,128]{1,0:T(8,128)S(1)} custom-call(f32[1024,128]{1,0:T(8,128)S(1)} %bitcast.6, f32[64,128]{1,0:T(8,128)S(1)} %bitcast.7, f32[64,128]{1,0:T(8,128)S(1)} %bitcast.8, f32[64,128]{1,0:T(8,128)S(1)} %bitcast.9), custom_call_target="tpu_custom_call" | custom-call | tf_op jit(solution)/shard_map/pallas_call | solution.py:297
  29.9 0.8 %copy.6 = f32[8,4,32,128]{3,2,1,0:T(8,128)} copy(f32[8,4,32,128]{3,2,1,0:T(8,128)S(1)} %bitcast.5) | data formatting | bytes 1048576
Async XLA Ops:
  0.0 1.0 %copy-start = (f32[8,4,32,128]{3,2,1,0:T(8,128)S(1)}, f32[8,4,32,128]{3,2,1,0:T(8,128)}, u32[]{:S(2)}) copy-start(f32[8,4,32,128]{3,2,1,0:T(8,128)} %param.4) | copy-start | bytes 1572868
  1.0 0.8 %copy-start.1 = (f32[2,1,32,128]{3,2,1,0:T(8,128)S(1)}, f32[2,1,32,128]{3,2,1,0:T(8,128)}, u32[]{:S(2)}) copy-start(f32[2,1,32,128]{3,2,1,0:T(8,128)} %param.5) | copy-start | bytes 98308
  1.8 0.8 %copy-start.2 = (f32[2,1,32,128]{3,2,1,0:T(8,128)S(1)}, f32[2,1,32,128]{3,2,1,0:T(8,128)}, u32[]{:S(2)}) copy-start(f32[2,1,32,128]{3,2,1,0:T(8,128)} %param.6) | copy-start | bytes 98308
  2.6 0.8 %copy-start.3 = (f32[2,1,32,128]{3,2,1,0:T(8,128)S(1)}, f32[2,1,32,128]{3,2,1,0:T(8,128)}, u32[]{:S(2)}) copy-start(f32[2,1,32,128]{3,2,1,0:T(8,128)} %param.7) | copy-start | bytes 98308
where the time goes:
time: 31.1 us; the launch traced here: 30.7 us
  Pallas kernels  26.6 us (86%)
  local copies, waits for them, and re-layouts  4.11 us (13%)
    pallas_call x1, Pallas kernels, on_device(): pl.pallas_call(functools.partial(kernel, n_lev, n_x, n_y, steps, tl, nlon...  26.6 us
    unnamed x9, local copies, waits for them, and re-layouts  4.11 us

commit v1 on v0

--- a/solution.py
+++ b/solution.py
@@ -66,8 +66,8 @@
     return part * rest, part * c
 
 
-def kernel(n_lev, n_x, n_y, steps, tl, nlon, x_ref, m_ref, fx_ref, fy_ref, o_ref,
-           dyn, eout, ein, edge, hxo, hxi, hyo, hyi, xs, qx, yb, yo,
+def kernel(n_lev, n_x, n_y, steps, tl, nlon, x_hbm, m_ref, fx_ref, fy_ref, o_ref,
+           x_ref, in_sem, dyn, eout, ein, edge, hxo, hxi, hyo, hyi, xs, qx, yb, yo,
            cf, cp, cq, ca, cb, mp, fp, mxs, myp, fyp, yp, yq, ya, ybt,
            d_s, d_r, ea_s, ea_r, eb_s, eb_r, hx_s, hx_r, hy_s, hy_r):
     z, gx, gy = lax.axis_index("tracer"), lax.axis_index("gx"), lax.axis_index("gy")
@@ -86,6 +86,15 @@
         return pltpu.make_async_remote_copy(src_ref=src, dst_ref=dst, send_sem=ss, recv_sem=rs,
                                             device_id=to, device_id_type=MESH)
 
+    loads = []
+    for s in range(steps):
+        for f, ref in enumerate((m_ref, fx_ref, fy_ref)):
+            loads.append(pltpu.make_async_copy(
+                ref.at[pl.ds(s * nlon, nlon)], dyn.at[s * n_lev + z, pl.ds(f * nlon, nlon)], in_sem.at[len(loads)]))
+            loads[-1].start()
+    load_x = pltpu.make_async_copy(x_hbm, x_ref, in_sem.at[len(loads)])
+    load_x.start()
+
     def pack_x(s, src):
         def body(lev, _):
             for c in range(H):
@@ -95,13 +104,17 @@
             return 0
         lax.fori_loop(0, n_lev, body, 0)
 
+    for copy in loads:
+        copy.wait()
     for s in range(steps):
-        for f, ref in enumerate((m_ref, fx_ref, fy_ref)):
-            dyn[s * n_lev + z, f * nlon:(f + 1) * nlon, :] = ref[s * nlon:(s + 1) * nlon, :]
-        eout[s * 4:s * 4 + 1, :] = m_ref[(s + 1) * nlon - 1:(s + 1) * nlon, :]
-        eout[s * 4 + 1:s * 4 + 2, :] = m_ref[s * nlon:s * nlon + 1, :]
-        eout[s * 4 + 2:s * 4 + 3, :] = fx_ref[s * nlon:s * nlon + 1, :]
-        eout[s * 4 + 3:s * 4 + 4, :] = fx_ref[s * nlon:s * nlon + 1, :]
+        own = s * n_lev + z
+        eout[s * 4:s * 4 + 1, :] = dyn[own, nlon - 1:nlon, :]
+        eout[s * 4 + 1:s * 4 + 2, :] = dyn[own, 0:1, :]
+        eout[s * 4 + 2:s * 4 + 3, :] = dyn[own, nlon:nlon + 1, :]
+        eout[s * 4 + 3:s * 4 + 4, :] = dyn[own, nlon:nlon + 1, :]
+    mp[0:SUB, :] = jnp.ones((SUB, LANES), jnp.float32)
+    fp[nlon:nlon + SUB, :] = jnp.zeros((SUB, LANES), jnp.float32)
+    load_x.wait()
     pack_x(0, x_ref)
     pl.semaphore_wait(barrier, len(who))
 
@@ -122,17 +135,17 @@
         go(remote(hxo.at[s, 0], hxi.at[s, 1], hx_s.at[s, 0], hx_r.at[s, 1], {"gx": left}))
         go(remote(hxo.at[s, 1], hxi.at[s, 0], hx_s.at[s, 1], hx_r.at[s, 0], {"gx": right}))
 
+    send_x(0)
     send_dyn(0)
-    send_x(0)
-    for side in range(2):
-        remote(eout, ein.at[side], ea_s.at[side], ea_r.at[side], {"gx": left}).wait_recv()
-    for s in range(steps):
-        edge[z, s * 4:s * 4 + 1, :] = ein[0, s * 4:s * 4 + 1, :]
-        edge[z, s * 4 + 1:s * 4 + 4, :] = ein[1, s * 4 + 1:s * 4 + 4, :]
-    for d, p in enumerate(peers):
-        go(remote(edge.at[z], edge.at[z], eb_s.at[d], eb_r.at[z], {"tracer": p}))
-    for s in range(1, steps):
-        send_dyn(s)
+
+    def share_edges():
+        for side in range(2):
+            remote(eout, ein.at[side], ea_s.at[side], ea_r.at[side], {"gx": left}).wait_recv()
+        for s in range(steps):
+            edge[z, s * 4:s * 4 + 1, :] = ein[0, s * 4:s * 4 + 1, :]
+            edge[z, s * 4 + 1:s * 4 + 4, :] = ein[1, s * 4 + 1:s * 4 + 4, :]
+        for d, p in enumerate(peers):
+            go(remote(edge.at[z], edge.at[z], eb_s.at[d], eb_r.at[z], {"tracer": p}))
 
     for s in range(steps):
         src = x_ref if s == 0 else xs
@@ -142,24 +155,22 @@
             lev = lax.rem(z + j, n_lev)
             slot = s * n_lev + lev
 
-            @pl.when(j > 0)
-            def _():
+            def here():
                 remote(dyn.at[slot], dyn.at[slot], d_s.at[s, 0], d_r.at[s, lev], {"tracer": z}).wait_recv()
-                if s == 0:
-                    remote(edge.at[lev], edge.at[lev], eb_s.at[0], eb_r.at[lev], {"tracer": z}).wait_recv()
+            if s > 0:
+                pl.when(j > 0)(here)
+            elif not isinstance(j, int):
+                here()
 
             m = dyn[slot, 0:nlon, :]
             mp[SUB:SUB + nlon, :] = m
-            mp[0:SUB, :] = jnp.broadcast_to(edge[lev, s * 4:s * 4 + 1, :], (SUB, LANES))
-            mp[SUB + nlon:2 * SUB + nlon, :] = jnp.broadcast_to(edge[lev, s * 4 + 1:s * 4 + 2, :], (SUB, LANES))
             fp[0:nlon, :] = dyn[slot, nlon:2 * nlon, :]
-            fp[nlon:nlon + SUB, :] = jnp.broadcast_to(edge[lev, s * 4 + 2:s * 4 + 3, :], (SUB, LANES))
-            f = fp[0:nlon + SUB, :]
-            pw, qw = face_weights(f, mp[SUB - 1:2 * SUB - 1 + nlon, :], mp[SUB:2 * SUB + nlon, :])
-            cf[lev] = f
-            cp[lev] = pw
-            cq[lev] = qw
-            mx = m - (fp[1:nlon + 1, :] - fp[0:nlon, :])
+            f = fp[0:nlon, :]
+            pw, qw = face_weights(f, mp[SUB - 1:SUB - 1 + nlon, :], m)
+            cf[lev, 0:nlon, :] = f
+            cp[lev, 0:nlon, :] = pw
+            cq[lev, 0:nlon, :] = qw
+            mx = m - (fp[1:nlon + 1, :] - f)
             inv = 1.0 / mx
             ca[lev] = m * inv
             cb[lev] = inv
@@ -175,12 +186,44 @@
         def put_x(base, i, v):
             qx[pl.ds(base + i, SUB, stride=nl), :] = v
 
-        lax.fori_loop(0, n_lev, x_inner, 0)
+        if s == 0:
+            x_inner(0, 0)
+            share_edges()
+            lax.fori_loop(1, n_lev, x_inner, 0)
+
+            def edge_here(j, _):
+                lev = lax.rem(z + j, n_lev)
+                remote(edge.at[lev], edge.at[lev], eb_s.at[0], eb_r.at[lev], {"tracer": z}).wait_recv()
+                return 0
+            lax.fori_loop(1, n_lev, edge_here, 0)
+            for later in range(1, steps):
+                send_dyn(later)
+        else:
+            lax.fori_loop(0, n_lev, x_inner, 0)
         for side in range(2):
             remote(hxo.at[s, 0], hxi.at[s, side], hx_s.at[s, side], hx_r.at[s, side], {"gx": left}).wait_recv()
 
         def x_edge(lev, _):
             base = lev * nlon
+            slot = s * n_lev + lev
+            first = slice(nlon, nlon + 1)
+            m_w = edge[lev, s * 4:s * 4 + 1, :]
+            m_e = edge[lev, s * 4 + 1:s * 4 + 2, :]
+            f_e = edge[lev, s * 4 + 2:s * 4 + 3, :]
+            f_w = dyn[slot, first, :]
+            pw, qw = face_weights(f_w, m_w, dyn[slot, 0:1, :])
+            cp[lev, 0:1, :] = pw
+            cq[lev, 0:1, :] = qw
+            m_last = dyn[slot, nlon - 1:nlon, :]
+            pw, qw = face_weights(f_e, m_last, m_e)
+            cf[lev, first, :] = f_e
+            cp[lev, first, :] = pw
+            cq[lev, first, :] = qw
+            mx = m_last - (f_e - dyn[slot, 2 * nlon - 1:2 * nlon, :])
+            inv = 1.0 / mx
+            ca[lev, nlon - 1:nlon, :] = m_last * inv
+            cb[lev, nlon - 1:nlon, :] = inv
+            mxs[pl.ds(base + nlon - 1, 1), :] = mx
 
             def q(i):
                 if i < 0:
@@ -205,7 +248,7 @@
             yb[pl.ds(off + t, LANES, stride=SUB), :] = jnp.transpose(
                 qx[pl.ds(pl.multiple_of(t * nl, nl), nl), :])
             return 0
-        lax.fori_loop(0, SUB, turn, 0)
+        lax.fori_loop(0, SUB, turn, 0, unroll=True)
         mt = jnp.transpose(mxs[...])
         ft = jnp.transpose(jnp.concatenate(
             [dyn[s * n_lev + lev, 2 * nlon:3 * nlon, :] for lev in range(n_lev)], axis=0))
@@ -276,7 +319,7 @@
         def back(t, _):
             dst[pl.ds(pl.multiple_of(t * nl, nl), nl), :] = jnp.transpose(yo[pl.ds(t, LANES, stride=SUB), :])
             return 0
-        lax.fori_loop(0, SUB, back, 0)
+        lax.fori_loop(0, SUB, back, 0, unroll=True)
         if s < steps - 1:
             pack_x(s + 1, xs)
             send_x(s + 1)
@@ -297,9 +340,10 @@
     out = pl.pallas_call(
         functools.partial(kernel, n_lev, n_x, n_y, steps, tl, nlon),
         out_shape=jax.ShapeDtypeStruct((rows, LANES), jnp.float32),
-        in_specs=[pl.BlockSpec(memory_space=pltpu.VMEM)] * 4,
+        in_specs=[pl.BlockSpec(memory_space=pltpu.HBM)] * 4,
         out_specs=pl.BlockSpec(memory_space=pltpu.VMEM),
         scratch_shapes=[
+            V(rows, LANES), dma(3 * steps + 1),
             V(steps * n_lev, 3 * nlon, LANES),
             V(SUB, LANES), V(2, SUB, LANES), V(n_lev, SUB, LANES),
             V(steps, 2, n_lev * H * SUB, LANES), V(steps, 2, n_lev * H * SUB, LANES),
@@ -314,7 +358,7 @@
             dma(steps, 2), dma(steps, 2), dma(steps, 2), dma(steps, 2),
         ],
         compiler_params=pltpu.CompilerParams(
-            collective_id=0, has_side_effects=True, vmem_limit_bytes=32 * 1024 * 1024),
+            collective_id=0, has_side_effects=True, vmem_limit_bytes=56 * 1024 * 1024),
     )(tracers.reshape(rows, LANES), air_mass.reshape(-1, LANES), flux_x.reshape(-1, LANES), flux_y.reshape(-1, LANES))
     return out.reshape(tracers.shape)
 

time: 31.1 us -> 24.7 us (0.79)
  Pallas kernels: 26.6 us -> 22.6 us
  local copies, waits for them, and re-layouts: 4.11 us -> 1.87 us
    pallas_call x1, Pallas kernels: 26.6 us -> 22.6 us  [on_device(): pl.pallas_call(functools.partial(kernel, n_lev, n_x, n_y, steps, tl, nlon...]
    unnamed x9 -> x1, local copies, waits for them, and re-layouts: 4.11 us -> 1.87 us
where the time goes in v1:
time: 24.7 us; the launch traced here: 24.5 us
  Pallas kernels  22.6 us (91%)
  local copies, waits for them, and re-layouts  1.87 us (8%)
    pallas_call x1, Pallas kernels, on_device(): pl.pallas_call(functools.partial(kernel, n_lev, n_x, n_y, steps, tl, nlon...  22.6 us
    unnamed x1, local copies, waits for them, and re-layouts  1.87 us

profile of v1, /device:TPU:0, one launch (start us, length us, event | category | flops | bytes accessed | tf_op | source)
XLA Modules:
  0.0 24.5 jit_solution(12746196580333309360)
XLA Ops:
  0.0 22.6 %shard_map.46 = f32[1024,128]{1,0:T(8,128)} custom-call(f32[1024,128]{1,0:T(8,128)} %bitcast.6, f32[64,128]{1,0:T(8,128)} %bitcast.7, f32[64,128]{1,0:T(8,128)} %bitcast.8, f32[64,128]{1,0:T(8,128)} %bitcast.9), custom_call_target="tpu_custom_call" | custom-call | tf_op jit(solution)/shard_map/pallas_call | solution.py:340
  22.6 1.9 %copy.6 = f32[8,4,32,128]{3,2,1,0:T(8,128)} copy(f32[8,4,32,128]{3,2,1,0:T(8,128)} %bitcast.5) | data formatting | bytes 1048576

commit v2 on v1

--- a/solution.py
+++ b/solution.py
@@ -102,7 +102,7 @@
                 hxo[s, 0, to, :] = src[pl.ds(lev * nlon + c, SUB, stride=nl), :]
                 hxo[s, 1, to, :] = src[pl.ds(lev * nlon + nlon - H + c, SUB, stride=nl), :]
             return 0
-        lax.fori_loop(0, n_lev, body, 0)
+        lax.fori_loop(0, n_lev, body, 0, unroll=True)
 
     for copy in loads:
         copy.wait()
@@ -240,20 +240,20 @@
                     functools.partial(put_x, base), a, b)
             return 0
 
-        lax.fori_loop(0, n_lev, x_edge, 0)
+        lax.fori_loop(0, n_lev, x_edge, 0, unroll=True)
 
         off = H * SUB
 
-        def turn(t, _):
-            yb[pl.ds(off + t, LANES, stride=SUB), :] = jnp.transpose(
-                qx[pl.ds(pl.multiple_of(t * nl, nl), nl), :])
-            return 0
-        lax.fori_loop(0, SUB, turn, 0, unroll=True)
         mt = jnp.transpose(mxs[...])
         ft = jnp.transpose(jnp.concatenate(
             [dyn[s * n_lev + lev, 2 * nlon:3 * nlon, :] for lev in range(n_lev)], axis=0))
         myp[SUB:SUB + LANES, :] = mt
         fyp[0:LANES, :] = ft
+
+        def turn(t, _):
+            yb[pl.ds(off + t, LANES, stride=SUB), :] = jnp.transpose(qx[t * nl:(t + 1) * nl, :])
+        for t in range(SUB):
+            turn(t, 0)
         extra = jnp.concatenate([mt[0:1], mt[LANES - 1:LANES], ft[0:1], ft[0:1], ft[0:1], ft[0:1], ft[0:1], ft[0:1]], axis=0)
         for side in range(2):
             hyo[s, side, H * SUB:(H + 1) * SUB, :] = extra
@@ -314,12 +314,12 @@
         def y_edge(b, _):
             y_rows(b * (LANES - SUB), SUB)
             return 0
-        lax.fori_loop(0, 2, y_edge, 0)
+        lax.fori_loop(0, 2, y_edge, 0, unroll=True)
 
         def back(t, _):
-            dst[pl.ds(pl.multiple_of(t * nl, nl), nl), :] = jnp.transpose(yo[pl.ds(t, LANES, stride=SUB), :])
-            return 0
-        lax.fori_loop(0, SUB, back, 0, unroll=True)
+            dst[t * nl:(t + 1) * nl, :] = jnp.transpose(yo[pl.ds(t, LANES, stride=SUB), :])
+        for t in range(SUB):
+            back(t, 0)
         if s < steps - 1:
             pack_x(s + 1, xs)
             send_x(s + 1)

time: 24.7 us -> 24.4 us (0.988)
  Pallas kernels: 22.6 us -> 22.3 us
    pallas_call x1, Pallas kernels: 22.6 us -> 22.3 us  [on_device(): pl.pallas_call(functools.partial(kernel, n_lev, n_x, n_y, steps, tl, nlon...]
where the time goes in v2:
time: 24.4 us; the launch traced here: 24.2 us
  Pallas kernels  22.3 us (91%)
  local copies, waits for them, and re-layouts  1.87 us (8%)
    pallas_call x1, Pallas kernels, on_device(): pl.pallas_call(functools.partial(kernel, n_lev, n_x, n_y, steps, tl, nlon...  22.3 us
    unnamed x1, local copies, waits for them, and re-layouts  1.87 us

profile of v2, /device:TPU:0, one launch (start us, length us, event | category | flops | bytes accessed | tf_op | source)
XLA Modules:
  0.0 24.2 jit_solution(1110753984608630350)
XLA Ops:
  0.0 22.3 %shard_map.46 = f32[1024,128]{1,0:T(8,128)} custom-call(f32[1024,128]{1,0:T(8,128)} %bitcast.6, f32[64,128]{1,0:T(8,128)} %bitcast.7, f32[64,128]{1,0:T(8,128)} %bitcast.8, f32[64,128]{1,0:T(8,128)} %bitcast.9), custom_call_target="tpu_custom_call" | custom-call | tf_op jit(solution)/shard_map/pallas_call | solution.py:340
  22.3 1.9 %copy.6 = f32[8,4,32,128]{3,2,1,0:T(8,128)} copy(f32[8,4,32,128]{3,2,1,0:T(8,128)} %bitcast.5) | data formatting | bytes 1048576

commit v3 on v2

--- a/solution.py
+++ b/solution.py
@@ -196,13 +196,13 @@
                 remote(edge.at[lev], edge.at[lev], eb_s.at[0], eb_r.at[lev], {"tracer": z}).wait_recv()
                 return 0
             lax.fori_loop(1, n_lev, edge_here, 0)
-            for later in range(1, steps):
-                send_dyn(later)
         else:
             lax.fori_loop(0, n_lev, x_inner, 0)
         for side in range(2):
             remote(hxo.at[s, 0], hxi.at[s, side], hx_s.at[s, side], hx_r.at[s, side], {"gx": left}).wait_recv()
 
+        for later in range(1, steps) if s == 0 else ():
+            send_dyn(later)
         def x_edge(lev, _):
             base = lev * nlon
             slot = s * n_lev + lev
@@ -284,9 +284,9 @@
             return put
 
         def y_inner(b, _):
-            y_rows(SUB + b * 16, 16)
-            return 0
-        lax.fori_loop(0, (LANES - 2 * SUB) // 16, y_inner, 0)
+            y_rows(SUB + b * 28, 28)
+            return 0
+        lax.fori_loop(0, (LANES - 2 * SUB) // 28, y_inner, 0)
 
         for side in range(2):
             remote(hyo.at[s, 0], hyi.at[s, side], hy_s.at[s, side], hy_r.at[s, side], {"gy": south}).wait_recv()

time: 24.4 us -> 24.4 us (level)
  no operation moved by 1% of the time
where the time goes in v3:
time: 24.4 us; the launch traced here: 24.2 us
  Pallas kernels  22.3 us (91%)
  local copies, waits for them, and re-layouts  1.87 us (8%)
    pallas_call x1, Pallas kernels, on_device(): pl.pallas_call(functools.partial(kernel, n_lev, n_x, n_y, steps, tl, nlon...  22.3 us
    unnamed x1, local copies, waits for them, and re-layouts  1.87 us

profile of v3, /device:TPU:0, one launch (start us, length us, event | category | flops | bytes accessed | tf_op | source)
XLA Modules:
  0.0 24.2 jit_solution(9114062781626725697)
XLA Ops:
  0.0 22.3 %shard_map.46 = f32[1024,128]{1,0:T(8,128)} custom-call(f32[1024,128]{1,0:T(8,128)} %bitcast.6, f32[64,128]{1,0:T(8,128)} %bitcast.7, f32[64,128]{1,0:T(8,128)} %bitcast.8, f32[64,128]{1,0:T(8,128)} %bitcast.9), custom_call_target="tpu_custom_call" | custom-call | tf_op jit(solution)/shard_map/pallas_call | solution.py:340
  22.3 1.9 %copy.6 = f32[8,4,32,128]{3,2,1,0:T(8,128)} copy(f32[8,4,32,128]{3,2,1,0:T(8,128)} %bitcast.5) | data formatting | bytes 1048576

commit v4 on v2

--- a/solution.py
+++ b/solution.py
@@ -71,7 +71,7 @@
            cf, cp, cq, ca, cb, mp, fp, mxs, myp, fyp, yp, yq, ya, ybt,
            d_s, d_r, ea_s, ea_r, eb_s, eb_r, hx_s, hx_r, hy_s, hy_r):
     z, gx, gy = lax.axis_index("tracer"), lax.axis_index("gx"), lax.axis_index("gy")
-    peers = [lax.rem(z + d, n_lev) for d in range(1, n_lev)]
+    peers = [lax.rem(z + n_lev - d, n_lev) for d in range(1, n_lev)]
     left, right = lax.rem(gx + n_x - 1, n_x), lax.rem(gx + 1, n_x)
     south, north = lax.rem(gy + n_y - 1, n_y), lax.rem(gy + 1, n_y)
     H = 3

time: 24.4 us -> 24.9 us (1.020)
  Pallas kernels: 22.3 us -> 22.8 us
    pallas_call x1, Pallas kernels: 22.3 us -> 22.8 us  [on_device(): pl.pallas_call(functools.partial(kernel, n_lev, n_x, n_y, steps, tl, nlon...]
where the time goes in v4:
time: 24.9 us; the launch traced here: 24.6 us
  Pallas kernels  22.8 us (92%)
  local copies, waits for them, and re-layouts  1.87 us (8%)
    pallas_call x1, Pallas kernels, on_device(): pl.pallas_call(functools.partial(kernel, n_lev, n_x, n_y, steps, tl, nlon...  22.8 us
    unnamed x1, local copies, waits for them, and re-layouts  1.87 us

profile of v4, /device:TPU:0, one launch (start us, length us, event | category | flops | bytes accessed | tf_op | source)
XLA Modules:
  0.0 24.6 jit_solution(4282000407991409252)
XLA Ops:
  0.0 22.8 %shard_map.46 = f32[1024,128]{1,0:T(8,128)} custom-call(f32[1024,128]{1,0:T(8,128)} %bitcast.6, f32[64,128]{1,0:T(8,128)} %bitcast.7, f32[64,128]{1,0:T(8,128)} %bitcast.8, f32[64,128]{1,0:T(8,128)} %bitcast.9), custom_call_target="tpu_custom_call" | custom-call | tf_op jit(solution)/shard_map/pallas_call | solution.py:340
  22.8 1.9 %copy.6 = f32[8,4,32,128]{3,2,1,0:T(8,128)} copy(f32[8,4,32,128]{3,2,1,0:T(8,128)} %bitcast.5) | data formatting | bytes 1048576
